TPU v7x, 256 devices: a whole 4x4x8 slice. The times are simulated.
256 devices in a mesh: mode: 32 (over y, z_hi, core), tm: 8 (over z_lo, x).
Axes of the slice: x: 4, y: 4, z: 8 (z_hi: 4, z_lo: 2; z = z_hi * 2 + z_lo), core: 2. Of those that a mesh axis runs over, the one named last changes fastest.
Arguments:
- envelope: bfloat16 [512, 2, 32768], P('mode', None, 'tm'), may hold values from -6 to 6
- mode_profile: bfloat16 [512, 8192], replicated, may hold values from -0.375 to 0.375
- dispersion: float32 [3, 512], P(None, 'mode'), may hold values from -0.5 to 0.5
- kerr_gain: float32 [512], replicated, may hold values from 0.03 to 0.12
Outputs:
- advanced: float32 [512, 2, 32768], P('mode', None, 'tm')
All inputs are finite; a program needn't handle non-finite values.
Results may differ from a plain program's by a relative error of at most 0.0027.
Values may be sent and summed in bfloat16 or wider, within the bound.
A program may use at most 64 MiB of HBM per device.

v0:
```python
import math

import jax
import jax.numpy as jnp
from jax import lax
from jax.sharding import PartitionSpec as P

FIRST_DIFF = (
    1.0 / 280,
    -4.0 / 105,
    1.0 / 5,
    -4.0 / 5,
    0.0,
    4.0 / 5,
    -1.0 / 5,
    4.0 / 105,
    -1.0 / 280,
)
SECOND_DIFF = (
    -1.0 / 560,
    8.0 / 315,
    -1.0 / 5,
    8.0 / 5,
    -205.0 / 72,
    8.0 / 5,
    -1.0 / 5,
    8.0 / 315,
    -1.0 / 560,
)
THIRD_DIFF = (
    7.0 / 240,
    -3.0 / 10,
    169.0 / 120,
    -61.0 / 30,
    0.0,
    61.0 / 30,
    -169.0 / 120,
    3.0 / 10,
    -7.0 / 240,
)


def padded_2(array, sides, width):
    for axis, dim in sides:
        devices, length = (lax.axis_size(axis), array.shape[dim])
        up = [(i, (i + 1) % devices) for i in range(devices)]
        down = [(j, i) for i, j in up]
        last = lax.slice_in_dim(array, length - width, length, axis=dim)
        leading = lax.slice_in_dim(array, 0, width, axis=dim)
        before = lax.ppermute(last, axis, up)
        after = lax.ppermute(leading, axis, down)
        array = jnp.concatenate([before, array, after], axis=dim)
    return array


def stencil_terms(padded, dispersion, samples):
    walk_off = dispersion[0][:, None]
    spread = dispersion[1][:, None]
    skewed = dispersion[2][:, None]
    real_out = jnp.zeros((padded.shape[0], samples), jnp.float32)
    imag_out = jnp.zeros((padded.shape[0], samples), jnp.float32)
    for offset in range(9):
        shifted = lax.slice_in_dim(padded, offset, offset + samples, axis=2)
        direct = -walk_off * FIRST_DIFF[offset] + skewed * (THIRD_DIFF[offset] / 6.0)
        crossed = spread * (SECOND_DIFF[offset] / 2.0)
        real_out = real_out + direct * shifted[:, 0] + crossed * shifted[:, 1]
        imag_out = imag_out + direct * shifted[:, 1] - crossed * shifted[:, 0]
    return jnp.stack([real_out, imag_out], 1)


def kerr_terms(block, mode_profile, kerr_gain):
    mode_count = block.shape[0]
    columns = block.shape[2]
    half_modes = mode_count // 2
    grid_points = mode_profile.shape[1]
    grid_block = math.gcd(grid_points, 2048)
    stacked = block.reshape(mode_count, 2 * columns)
    field_pair = (stacked[:half_modes], stacked[half_modes:])

    def accumulate(running, block_index):
        profile_block = lax.dynamic_slice_in_dim(
            mode_profile, block_index * grid_block, grid_block, 1
        )
        profile_pair = (profile_block[:half_modes], profile_block[half_modes:])
        grid_fields = [
            lax.dot_general(
                profile_pair[which_pol],
                field_pair[which_pol],
                (((0,), (0,)), ((), ())),
                preferred_element_type=jnp.float32,
            ).reshape(grid_block, 2, columns)
            for which_pol in (0, 1)
        ]
        intensity = (
            grid_fields[0][:, 0] ** 2
            + grid_fields[0][:, 1] ** 2
            + grid_fields[1][:, 0] ** 2
            + grid_fields[1][:, 1] ** 2
        )
        cubic_pair = [
            (intensity[:, None, :] * grid_field)
            .astype(jnp.bfloat16)
            .reshape(grid_block, 2 * columns)
            for grid_field in grid_fields
        ]
        projected = jnp.concatenate(
            [
                jnp.dot(
                    profile_pair[which_pol],
                    cubic_pair[which_pol],
                    preferred_element_type=jnp.float32,
                )
                for which_pol in (0, 1)
            ],
            0,
        )
        return (running + projected, None)

    running, unused = lax.scan(
        accumulate,
        jnp.zeros((mode_count, 2 * columns), jnp.float32),
        jnp.arange(grid_points // grid_block, dtype=jnp.int32),
    )
    summed = running.reshape(mode_count, 2, columns)
    kerr_scale = (kerr_gain * (half_modes / grid_points))[:, None]
    return jnp.stack([-kerr_scale * summed[:, 1], kerr_scale * summed[:, 0]], 1)


def dispersion_terms(signal, dispersion):
    padded = padded_2(signal, (("tm", 2),), 4).astype(jnp.float32)
    return stencil_terms(padded, dispersion, signal.shape[2])


def split_blocks(signal, count):
    return signal.reshape(signal.shape[0], signal.shape[1], count, signal.shape[2] // count)


def on_device(envelope, mode_profile, dispersion, kerr_gain):

    def kerr_local(block):
        return kerr_terms(block, mode_profile, kerr_gain)

    def kerr_items(items):
        flat = items.reshape(items.shape[0], items.shape[1], items.shape[3])
        result = kerr_local(flat)
        return result.reshape(result.shape[0], result.shape[1], 1, result.shape[2])

    count = lax.axis_size("mode")
    local_modes = envelope.shape[0]
    samples = envelope.shape[2]
    initial = envelope.astype(jnp.float32)

    def kerr_round(signal):
        remote = kerr_items(
            lax.all_to_all(
                split_blocks(signal, count), "mode", split_axis=2, concat_axis=0, tiled=True
            )
        )
        back = lax.all_to_all(remote, "mode", split_axis=0, concat_axis=2, tiled=True)
        return back.reshape(local_modes, 2, samples)

    first_rate = dispersion_terms(envelope, dispersion) + kerr_round(envelope)
    midway = (initial + first_rate).astype(jnp.bfloat16)
    second_rate = dispersion_terms(midway, dispersion) + kerr_round(midway)
    return initial + 0.5 * (first_rate + second_rate)


def solution(mesh):
    placed = (P("mode", None, "tm"), P(), P(None, "mode"), P())
    return jax.shard_map(
        on_device, mesh=mesh, in_specs=placed, out_specs=P("mode", None, "tm"), check_vma=False
    )
```

profile of v0, /device:TPU:1, one launch (start us, length us, event | category | flops | bytes accessed | tf_op | source)
XLA Modules:
  0.0 173.4 jit_solution(17629374406369623136)
XLA Ops:
  0.0 1.8 %copy_bitcast_fusion.1 = bf16[16,2,32,128]{3,1,0,2:T(2,128)(2,1)} fusion(bf16[16,2,4096]{2,1,0:T(2,128)(2,1)} %param.8), kind=kLoop, calls=%fused_computation.56 | loop fusion | bytes 524288 | tf_op jit(solution)/shard_map/reshape | solution.py:135
  1.8 12.8 %all-to-all-start = ((bf16[16,2,32,128]{3,1,0,2:T(2,128)(2,1)}), bf16[16,2,32,128]{3,1,0,2:T(2,128)(2,1)S(1)}, u32[]{:S(2)}, u32[]{:S(2)}) async-start(bf16[16,2,32,128]{3,1,0,2:T(2,128)(2,1)} %copy_bitcast_fusion.1), calls=%async_computation | async-start | bytes 524288 | tf_op jit(solution)/shard_map/all_to_all | solution.py:155
  15.8 1.2 collective-permute-start
  17.0 2.4 %collective-permute-start.1 = (bf16[16,2,4]{2,0,1:T(8,128)(2,1)S(1)}, bf16[16,2,4]{2,0,1:T(8,128)(2,1)S(1)}, u32[]{:S(2)}, u32[]{:S(2)}) collective-permute-start(bf16[16,2,4]{2,0,1:T(8,128)(2,1)S(1)} %get-tuple-element.149), channel_id=1, source_target_pairs={{1,0},{2,1},{3,2},{4,3},{5,4},{6,5},{7,6},{0,7},{9,8},{10,9},{11,1... | collective-permute-start | bytes 776 | tf_op jit(solution)/shard_map/ppermute | solution.py:51
  21.7 1.5 collective-permute-done
  23.4 4.6 %all-to-all-done = bf16[16,2,32,128]{3,1,0,2:T(2,128)(2,1)S(1)} async-done(((bf16[16,2,32,128]{3,1,0,2:T(2,128)(2,1)}), bf16[16,2,32,128]{3,1,0,2:T(2,128)(2,1)S(1)}, u32[]{:S(2)}, u32[]{:S(2)}) %all-to-all-start) | async-done | bytes 262176 | tf_op jit(solution)/shard_map/all_to_all | solution.py:155
  28.2 36.9 %while.22 = (s32[]{:T(128)}, f32[512,256]{1,0:T(8,128)S(1)}, s32[4]{0:T(128)S(1)}, bf16[512,8192]{1,0:T(8,128)(2,1)}, bf16[256,256]{1,0:T(8,128)(2,1)S(1)}, /*in...) while((s32[]{:T(128)}, f32[512,256]{1,0:T(8,128)S(1)}, ...), condition=%wide.region_1.2_spmd.clone, body=%wide.region_0.1_spmd.clone.sunk | while | flops 1078067200 | bytes 25428188 | solution.py:119
  29.5 1.7 fusion.86
  31.2 1.7 fusion.87
  33.9 1.7 fusion.90
  35.6 1.7 fusion.91
  38.7 1.7 fusion.86
  40.4 1.7 fusion.87
  43.1 1.7 fusion.90
  44.8 1.7 fusion.91
  47.9 1.7 fusion.86
  49.6 1.7 fusion.87
  52.3 1.7 fusion.90
  54.0 1.7 fusion.91
  57.1 1.7 fusion.86
  58.9 1.7 fusion.87
  61.5 1.7 fusion.90
  63.2 1.7 fusion.91
  66.4 6.4 %all-to-all-start.1 = ((f32[512,2,1,128]{3,1,2,0:T(2,128)}), f32[512,2,1,128]{3,1,2,0:T(2,128)S(1)}, u32[]{:S(2)}, u32[]{:S(2)}) async-start(f32[512,2,1,128]{3,1,2,0:T(2,128)} %copy.46), calls=%async_computation.1 | async-start | bytes 1048576 | tf_op jit(solution)/shard_map/all_to_all | solution.py:159
  75.2 15.5 %all-to-all-done.1 = f32[512,2,1,128]{3,1,2,0:T(2,128)S(1)} async-done(((f32[512,2,1,128]{3,1,2,0:T(2,128)}), f32[512,2,1,128]{3,1,2,0:T(2,128)S(1)}, u32[]{:S(2)}, u32[]{:S(2)}) %all-to-all-start.1) | async-done | bytes 524320 | tf_op jit(solution)/shard_map/all_to_all | solution.py:159
  92.0 4.9 %all-to-all-start.2 = ((bf16[16,2,32,128]{3,0,1,2:T(8,128)(2,1)}), bf16[16,2,32,128]{3,0,1,2:T(8,128)(2,1)S(1)}, u32[]{:S(2)}, u32[]{:S(2)}) async-start(bf16[16,2,32,128]{3,0,1,2:T(8,128)(2,1)} %copy_bitcast_fusion), calls=%async_computation.2 | async-start | bytes 524288 | tf_op jit(solution)/shard_map/all_to_all | solution.py:155
  97.0 3.6 %collective-permute-start.3 = (bf16[16,2,4]{2,0,1:T(8,128)(2,1)S(1)}, bf16[16,2,4]{2,0,1:T(8,128)(2,1)S(1)}, u32[]{:S(2)}, u32[]{:S(2)}) collective-permute-start(bf16[16,2,4]{2,0,1:T(8,128)(2,1)S(1)} %get-tuple-element.145), channel_id=1, source_target_pairs={{1,0},{2,1},{3,2},{4,3},{5,4},{6,5},{7,6},{0,7},{9,8},{10,9},{11,1... | collective-permute-start | bytes 776 | tf_op jit(solution)/shard_map/ppermute | solution.py:51
  100.6 2.7 %collective-permute-done.2 = bf16[16,2,4]{2,0,1:T(8,128)(2,1)S(1)} collective-permute-done((bf16[16,2,4]{2,0,1:T(8,128)(2,1)S(1)}, bf16[16,2,4]{2,0,1:T(8,128)(2,1)S(1)}, u32[]{:S(2)}, u32[]{:S(2)}) %collective-permute-start.2) | collective-permute-done | bytes 288 | tf_op jit(solution)/shard_map/ppermute | solution.py:50
  103.6 6.6 %all-to-all-done.2 = bf16[16,2,32,128]{3,0,1,2:T(8,128)(2,1)S(1)} async-done(((bf16[16,2,32,128]{3,0,1,2:T(8,128)(2,1)}), bf16[16,2,32,128]{3,0,1,2:T(8,128)(2,1)S(1)}, u32[]{:S(2)}, u32[]{:S(2)}) %all-to-all-start.2) | async-done | bytes 262176 | tf_op jit(solution)/shard_map/all_to_all | solution.py:155
  110.5 36.9 %while.23 = (s32[]{:T(128)}, f32[512,256]{1,0:T(8,128)S(1)}, s32[4]{0:T(128)S(1)}, bf16[512,8192]{1,0:T(8,128)(2,1)}, bf16[256,256]{1,0:T(8,128)(2,1)S(1)}, /*in...) while((s32[]{:T(128)}, f32[512,256]{1,0:T(8,128)S(1)}, ...), condition=%wide.region_3.4_spmd.clone, body=%wide.region_2.3_spmd.clone.sunk | while | flops 1078067200 | bytes 25428188 | solution.py:119
  111.7 1.7 fusion.100
  113.4 1.7 fusion.101
  116.1 1.7 fusion.104
  117.8 1.7 fusion.105
  120.9 1.7 fusion.100
  122.7 1.7 fusion.101
  125.3 1.7 fusion.104
  127.0 1.7 fusion.105
  130.2 1.7 fusion.100
  131.9 1.7 fusion.101
  134.5 1.7 fusion.104
  136.3 1.7 fusion.105
  139.4 1.7 fusion.100
  141.1 1.7 fusion.101
  143.8 1.7 fusion.104
  145.5 1.7 fusion.105
  148.6 4.9 %all-to-all-start.3 = ((f32[512,2,1,128]{3,1,2,0:T(2,128)}), f32[512,2,1,128]{3,1,2,0:T(2,128)S(1)}, u32[]{:S(2)}, u32[]{:S(2)}) async-start(f32[512,2,1,128]{3,1,2,0:T(2,128)} %copy.53), calls=%async_computation.3 | async-start | bytes 1048576 | tf_op jit(solution)/shard_map/all_to_all | solution.py:159
  155.9 15.7 %all-to-all-done.3 = f32[512,2,1,128]{3,1,2,0:T(2,128)S(1)} async-done(((f32[512,2,1,128]{3,1,2,0:T(2,128)}), f32[512,2,1,128]{3,1,2,0:T(2,128)S(1)}, u32[]{:S(2)}, u32[]{:S(2)}) %all-to-all-start.3) | async-done | bytes 524320 | tf_op jit(solution)/shard_map/all_to_all | solution.py:159
  (94 shorter events, 28.3 us)
Async XLA Ops:
  1.8 26.2 %all-to-all-start = ((bf16[16,2,32,128]{3,1,0,2:T(2,128)(2,1)}), bf16[16,2,32,128]{3,1,0,2:T(2,128)(2,1)S(1)}, u32[]{:S(2)}, u32[]{:S(2)}) async-start(bf16[16,2,32,128]{3,1,0,2:T(2,128)(2,1)} %copy_bitcast_fusion.1), calls=%async_computation | async-start | bytes 524288 | tf_op jit(solution)/shard_map/all_to_all | solution.py:155
  15.8 7.3 %collective-permute-start = (bf16[16,2,4]{2,0,1:T(8,128)(2,1)S(1)}, bf16[16,2,4]{2,0,1:T(8,128)(2,1)S(1)}, u32[]{:S(2)}, u32[]{:S(2)}) collective-permute-start(bf16[16,2,4]{2,0,1:T(8,128)(2,1)S(1)} %get-tuple-element.150), channel_id=1, source_target_pairs={{0,1},{1,2},{2,3},{3,4},{4,5},{5,6},{6,7},{7,0},{8,9},{9,10},{10,1... | collective-permute-start | bytes 776 | tf_op jit(solution)/shard_map/ppermute | solution.py:50
  17.0 6.1 %collective-permute-start.1 = (bf16[16,2,4]{2,0,1:T(8,128)(2,1)S(1)}, bf16[16,2,4]{2,0,1:T(8,128)(2,1)S(1)}, u32[]{:S(2)}, u32[]{:S(2)}) collective-permute-start(bf16[16,2,4]{2,0,1:T(8,128)(2,1)S(1)} %get-tuple-element.149), channel_id=1, source_target_pairs={{1,0},{2,1},{3,2},{4,3},{5,4},{6,5},{7,6},{0,7},{9,8},{10,9},{11,1... | collective-permute-start | bytes 776 | tf_op jit(solution)/shard_map/ppermute | solution.py:51
  66.4 24.3 %all-to-all-start.1 = ((f32[512,2,1,128]{3,1,2,0:T(2,128)}), f32[512,2,1,128]{3,1,2,0:T(2,128)S(1)}, u32[]{:S(2)}, u32[]{:S(2)}) async-start(f32[512,2,1,128]{3,1,2,0:T(2,128)} %copy.46), calls=%async_computation.1 | async-start | bytes 1048576 | tf_op jit(solution)/shard_map/all_to_all | solution.py:159
  74.0 17.0 %copy-start.4 = (f32[16,1,4096]{2,0,1:T(8,128)}, f32[16,1,4096]{2,0,1:T(8,128)S(1)}, u32[]{:S(2)}) copy-start(f32[16,1,4096]{2,0,1:T(8,128)S(1)} %multiply_subtract_fusion.1) | copy-start | bytes 786436
  75.2 16.0 %copy-start.6 = (f32[16,1,4096]{2,0,1:T(8,128)}, f32[16,1,4096]{2,0,1:T(8,128)S(1)}, u32[]{:S(2)}) copy-start(f32[16,1,4096]{2,0,1:T(8,128)S(1)} %multiply_add_fusion.1) | copy-start | bytes 786436
  75.2 15.8 %copy-start.2 = (bf16[16,2,4096]{2,1,0:T(2,128)(2,1)S(1)}, bf16[16,2,4096]{2,1,0:T(2,128)(2,1)}, u32[]{:S(2)}) copy-start(bf16[16,2,4096]{2,1,0:T(2,128)(2,1)} %param.8) | copy-start | bytes 786436
  91.0 19.2 %copy-start = (f32[16,2,4096]{2,0,1:T(8,128)}, f32[16,2,4096]{2,0,1:T(8,128)S(1)}, u32[]{:S(2)}) copy-start(f32[16,2,4096]{2,0,1:T(8,128)S(1)} %reshape.733) | copy-start | bytes 1572868
  92.0 18.2 %all-to-all-start.2 = ((bf16[16,2,32,128]{3,0,1,2:T(8,128)(2,1)}), bf16[16,2,32,128]{3,0,1,2:T(8,128)(2,1)S(1)}, u32[]{:S(2)}, u32[]{:S(2)}) async-start(bf16[16,2,32,128]{3,0,1,2:T(8,128)(2,1)} %copy_bitcast_fusion), calls=%async_computation.2 | async-start | bytes 524288 | tf_op jit(solution)/shard_map/all_to_all | solution.py:155
  97.0 6.3 %collective-permute-start.2 = (bf16[16,2,4]{2,0,1:T(8,128)(2,1)S(1)}, bf16[16,2,4]{2,0,1:T(8,128)(2,1)S(1)}, u32[]{:S(2)}, u32[]{:S(2)}) collective-permute-start(bf16[16,2,4]{2,0,1:T(8,128)(2,1)S(1)} %get-tuple-element.146), channel_id=1, source_target_pairs={{0,1},{1,2},{2,3},{3,4},{4,5},{5,6},{6,7},{7,0},{8,9},{9,10},{10,1... | collective-permute-start | bytes 776 | tf_op jit(solution)/shard_map/ppermute | solution.py:50
  97.0 6.2 %collective-permute-start.3 = (bf16[16,2,4]{2,0,1:T(8,128)(2,1)S(1)}, bf16[16,2,4]{2,0,1:T(8,128)(2,1)S(1)}, u32[]{:S(2)}, u32[]{:S(2)}) collective-permute-start(bf16[16,2,4]{2,0,1:T(8,128)(2,1)S(1)} %get-tuple-element.145), channel_id=1, source_target_pairs={{1,0},{2,1},{3,2},{4,3},{5,4},{6,5},{7,6},{0,7},{9,8},{10,9},{11,1... | collective-permute-start | bytes 776 | tf_op jit(solution)/shard_map/ppermute | solution.py:51
  148.6 23.0 %all-to-all-start.3 = ((f32[512,2,1,128]{3,1,2,0:T(2,128)}), f32[512,2,1,128]{3,1,2,0:T(2,128)S(1)}, u32[]{:S(2)}, u32[]{:S(2)}) async-start(f32[512,2,1,128]{3,1,2,0:T(2,128)} %copy.53), calls=%async_computation.3 | async-start | bytes 1048576 | tf_op jit(solution)/shard_map/all_to_all | solution.py:159
  155.9 16.0 %copy-start.1 = (f32[16,2,4096]{2,0,1:T(8,128)S(1)}, f32[16,2,4096]{2,0,1:T(8,128)}, u32[]{:S(2)}) copy-start(f32[16,2,4096]{2,0,1:T(8,128)} %copy-done) | copy-start | bytes 1572868
  155.9 16.0 %copy-start.3 = (bf16[16,2,4096]{2,1,0:T(2,128)(2,1)S(1)}, bf16[16,2,4096]{2,1,0:T(2,128)(2,1)}, u32[]{:S(2)}) copy-start(bf16[16,2,4096]{2,1,0:T(2,128)(2,1)} %param.8) | copy-start | bytes 786436
  155.9 16.0 %copy-start.5 = (f32[16,1,4096]{2,0,1:T(8,128)S(1)}, f32[16,1,4096]{2,0,1:T(8,128)}, u32[]{:S(2)}) copy-start(f32[16,1,4096]{2,0,1:T(8,128)} %copy-done.4) | copy-start | bytes 786436
  155.9 16.0 %copy-start.7 = (f32[16,1,4096]{2,0,1:T(8,128)S(1)}, f32[16,1,4096]{2,0,1:T(8,128)}, u32[]{:S(2)}) copy-start(f32[16,1,4096]{2,0,1:T(8,128)} %copy-done.6) | copy-start | bytes 786436
where the time goes:
time: 175 us; the launch traced here: 173 us
  matrix products  54.6 us (31%)
  waiting for transfers between devices  46.4 us (27%)
  starting transfers between devices  36.1 us (21%)
  other arithmetic  16.4 us (9%)
  local copies, waits for them, and re-layouts  13.7 us (8%)
  loops' own time  5.79 us (3%)
    all_to_all x2, waiting for transfers between devices, kerr_round(): lax.all_to_all(remote, 'mode', split_axis=0, concat_axis=2, tiled=True)  31.2 us
    dot_general x16, matrix products, accumulate(): lax.dot_general(profile_pair[which_pol], field_pair[which_pol], (((0,), (...  27.3 us
    dot_general x16, matrix products, accumulate(): jnp.dot(profile_pair[which_pol], cubic_pair[which_pol], preferred_element...  27.2 us
    all_to_all x2, starting transfers between devices, kerr_round(): lax.all_to_all(split_blocks(signal, count), 'mode', split_axis=2, concat_...  17.7 us
    all_to_all x2, starting transfers between devices, kerr_round(): lax.all_to_all(remote, 'mode', split_axis=0, concat_axis=2, tiled=True)  11.2 us
    all_to_all x2, waiting for transfers between devices, kerr_round(): lax.all_to_all(split_blocks(signal, count), 'mode', split_axis=2, concat_...  11.1 us
    ppermute x2, starting transfers between devices, padded_2(): after = lax.ppermute(leading, axis, down)  5.93 us
    another operation x2, loops' own time, kerr_terms(): lax.scan(accumulate, jnp.zeros((mode_count, 2 * columns), jnp.float32), j...  5.79 us
  transfers between devices with their start and end apart: 8, of which 6 were waited for; matrix products, arithmetic and copies ran while one was open for 5% of the time, Pallas kernels for 0%

commit v1 on v0

v1 whole, which is shorter than its diff:
```python
import functools

import jax
import jax.numpy as jnp
import ml_dtypes
import numpy as np
from jax import lax
from jax.experimental import pallas as pl
from jax.experimental.pallas import tpu as pltpu
from jax.sharding import PartitionSpec as P

FIRST_DIFF = (1.0 / 280, -4.0 / 105, 1.0 / 5, -4.0 / 5, 0.0, 4.0 / 5, -1.0 / 5, 4.0 / 105, -1.0 / 280)
SECOND_DIFF = (-1.0 / 560, 8.0 / 315, -1.0 / 5, 8.0 / 5, -205.0 / 72, 8.0 / 5, -1.0 / 5, 8.0 / 315, -1.0 / 560)
THIRD_DIFF = (7.0 / 240, -3.0 / 10, 169.0 / 120, -61.0 / 30, 0.0, 61.0 / 30, -169.0 / 120, 3.0 / 10, -7.0 / 240)

MESH = pl.DeviceIdType.MESH
F32, BF16 = jnp.float32, jnp.bfloat16
NT = (((1,), (1,)), ((), ()))
TN = (((0,), (0,)), ((), ()))
W = 128


def hi_lo(x):
    hi = x.astype(ml_dtypes.bfloat16)
    lo = (x - hi.astype(np.float64)).astype(ml_dtypes.bfloat16)
    return hi, lo


def constants():
    taps = (np.array(FIRST_DIFF), np.array(SECOND_DIFF) / 2, np.array(THIRD_DIFF) / 6)
    main = np.zeros((W, 3 * W))
    halo = np.zeros((32, 6 * W))
    for which, tap in enumerate(taps):
        for t in range(W):
            for k in range(-4, 5):
                s, col = t + k, which * W + t
                if 0 <= s < W:
                    main[s, col] = tap[k + 4]
                else:
                    row = s + 4 if s < 0 else 16 + s - W
                    halo[row, col] = tap[k + 4]
                    halo[row + 4, 3 * W + col] = tap[k + 4]
    pick = np.zeros((32, 2 * W))
    for j in range(4):
        pick[j, j] = pick[4 + j, W + j] = 1
        pick[16 + j, W - 4 + j] = pick[20 + j, 2 * W - 4 + j] = 1
    return np.concatenate(hi_lo(main), 0), np.concatenate(hi_lo(halo), 0), pick.astype(ml_dtypes.bfloat16)


def dot(a, b, dims=(((1,), (0,)), ((), ()))):
    return lax.dot_general(a, b, dims, preferred_element_type=F32)


def kernel(
    peers, count, env_ref, prof_ref, disp_ref, gain_ref, main_ref, halo_ref, pick_ref, back_ref,
    env, prof, proft, field, mid, first, proj, sendbuf, incr, edges, halos, disp, drow, dall, coef,
    lsem, psem, ssem, rsem, dssem, drsem, hssem, hrsem, bssem, brsem,
):
    me, tm = lax.axis_index("mode"), lax.axis_index("tm")
    slabs = lax.axis_size("tm")
    grid = prof.shape[1]
    parts = psem.shape[0]
    width = grid // parts

    def to(peer):
        dy, dz, dc = peer
        y, z, c = me // 8, (me // 2) % 4, me % 2
        return ((y + dy) % 4) * 8 + ((z + dz) % 4) * 2 + (c + dc) % 2

    right = (lax.rem(me + 1, count), lax.rem(tm + (me + 1) // count, slabs))
    left = (lax.rem(me + count - 1, count), lax.rem(tm + slabs - (count - me) // count, slabs))

    barrier = pltpu.get_barrier_semaphore()
    for peer in peers:
        pl.semaphore_signal(barrier, inc=1, device_id=(to(peer), tm), device_id_type=MESH)
    for who in (left, right):
        pl.semaphore_signal(barrier, inc=1, device_id=who, device_id_type=MESH)

    env_in = pltpu.make_async_copy(env_ref, env, lsem.at[0])
    env_in.start()
    disp_in = pltpu.make_async_copy(disp_ref, disp, lsem.at[1])
    disp_in.start()

    def prof_in(i):
        cols = pl.ds(i * width, width)
        return pltpu.make_async_copy(prof_ref.at[:, cols], prof.at[:, cols], psem.at[i])

    for i in range(parts):
        prof_in(i).start()

    env_in.wait()
    for k in range(count):
        block = env[:, :, k * W : (k + 1) * W]
        sendbuf[k, :, 0:W] = block[:, 0, :]
        sendbuf[k, :, W : 2 * W] = block[:, 1, :]
    disp_in.wait()
    drow[...] = jnp.zeros_like(drow)
    drow[0:3, 0:16] = disp[...]
    rows = drow[...]
    packed = rows[0:1] + pltpu.roll(rows[1:2], 16, 1) + pltpu.roll(rows[2:3], 32, 1)
    dall[me] = packed

    pl.semaphore_wait(barrier, len(peers) + 2)

    my_rows = pl.ds(pl.multiple_of(me * 16, 16), 16)
    own = pltpu.make_async_copy(sendbuf.at[me], field.at[my_rows, :], lsem.at[2])
    own.start()
    sends, dsends = [], []
    for j, peer in enumerate(peers):
        sends.append(pltpu.make_async_remote_copy(
            src_ref=sendbuf.at[to(peer)], dst_ref=field.at[my_rows, :], send_sem=ssem.at[j], recv_sem=rsem.at[j],
            device_id=(to(peer), tm), device_id_type=MESH))
        sends[-1].start()
    for j, peer in enumerate(peers):
        dsends.append(pltpu.make_async_remote_copy(
            src_ref=dall.at[me], dst_ref=dall.at[me], send_sem=dssem.at[j], recv_sem=drsem.at[j],
            device_id=(to(peer), tm), device_id_type=MESH))
        dsends[-1].start()

    unit = (lax.broadcasted_iota(jnp.int32, (256, 256), 0) == lax.broadcasted_iota(jnp.int32, (256, 256), 1)).astype(BF16)
    for i in range(parts):
        prof_in(i).wait()

        def flip(b, _, i=i):
            at = pl.ds(pl.multiple_of(i * width + b * 256, 256), 256)
            for q in (0, 1):
                proft[at, 256 * q : 256 * q + 256] = dot(unit, prof[256 * q : 256 * q + 256, at], NT).astype(BF16)
            return 0

        lax.fori_loop(0, width // 256, flip, 0, unroll=True)

    diagonal = lax.broadcasted_iota(jnp.int32, (W, W), 0) == lax.broadcasted_iota(jnp.int32, (W, W), 1)
    for r in range(4):
        picked = jnp.where(diagonal, gain_ref[r : r + 1, :] * (256.0 / grid), 0.0)
        coef[3, r * W : (r + 1) * W, :] = jnp.broadcast_to(jnp.sum(picked, 1, keepdims=True), (W, W))

    own.wait()
    for cp in sends:
        cp.wait_send()
    for cp in sends:
        cp.wait_recv()

    def send_edges(values, turn):
        edges[turn] = dot(pick_ref[...], values, NT).astype(BF16).reshape(2, 16, 512)
        out = []
        for side, who in ((0, left), (1, right)):
            out.append(pltpu.make_async_remote_copy(
                src_ref=edges.at[turn, side], dst_ref=halos.at[turn, 1 - side], send_sem=hssem.at[turn, side],
                recv_sem=hrsem.at[turn, 1 - side], device_id=who, device_id_type=MESH))
            out[-1].start()
        return out

    hsends = send_edges(field[...], 0)
    for cp in dsends:
        cp.wait_send()
    for cp in dsends:
        cp.wait_recv()
    lane, sub = (lax.broadcasted_iota(jnp.int32, (16, W), d) for d in (1, 0))
    for i in range(count):
        row = jnp.broadcast_to(dall[i], (16, W))
        for d in range(3):
            column = jnp.sum(jnp.where(lane == sub + 16 * d, row, 0.0), 1, keepdims=True)
            coef[d, 16 * i : 16 * i + 16, :] = jnp.broadcast_to(column, (16, W))

    def kerr(src):
        step = 2048
        for b in range(grid // step):
            at = slice(b * step, (b + 1) * step)
            g = [dot(proft[at, 256 * q : 256 * q + 256], src[256 * q : 256 * q + 256, :]) for q in (0, 1)]
            level = g[0][:, :W] ** 2 + g[0][:, W:] ** 2 + g[1][:, :W] ** 2 + g[1][:, W:] ** 2
            level = jnp.concatenate([level, level], 1)
            for q in (0, 1):
                part = dot(prof[256 * q : 256 * q + 256, at], (level * g[q]).astype(BF16))
                if b == 0:
                    proj[256 * q : 256 * q + 256, :] = part
                else:
                    proj[256 * q : 256 * q + 256, :] += part

    def rate(src, turn):
        values = src[...]
        re, im = values[:, :W], values[:, W:]
        side = halos[turn].reshape(32, 512).astype(F32).T.astype(BF16)
        side = dot(jnp.concatenate([side, side], 1), halo_ref[...])
        d_re = dot(jnp.concatenate([re, re], 1), main_ref[...]) + side[:, : 3 * W]
        d_im = dot(jnp.concatenate([im, im], 1), main_ref[...]) + side[:, 3 * W :]
        walk, spread, skew, kerr_gain = coef[0], coef[1], coef[2], coef[3]
        out_re = skew * d_re[:, 2 * W :] - walk * d_re[:, :W] + spread * d_im[:, W : 2 * W] - kerr_gain * proj[:, W:]
        out_im = skew * d_im[:, 2 * W :] - walk * d_im[:, :W] - spread * d_re[:, W : 2 * W] + kerr_gain * proj[:, :W]
        return jnp.concatenate([out_re, out_im], 1)

    def wait_edges(copies):
        for cp in copies:
            cp.wait_send()
        for cp in copies:
            cp.wait_recv()

    kerr(field)
    wait_edges(hsends)
    first[...] = rate(field, 0)
    mid[...] = (field[...].astype(F32) + first[...]).astype(BF16)
    hsends = send_edges(mid[...], 1)
    kerr(mid)
    wait_edges(hsends)
    incr[...] = (0.5 * (first[...] + rate(mid, 1))).astype(BF16)

    own = pltpu.make_async_copy(incr.at[my_rows, :], back_ref.at[me], lsem.at[3])
    own.start()
    sends = []
    for j, peer in enumerate(peers):
        sends.append(pltpu.make_async_remote_copy(
            src_ref=incr.at[pl.ds(pl.multiple_of(to(peer) * 16, 16), 16), :], dst_ref=back_ref.at[me],
            send_sem=bssem.at[j], recv_sem=brsem.at[j], device_id=(to(peer), tm), device_id_type=MESH))
        sends[-1].start()
    own.wait()
    for cp in sends:
        cp.wait_send()
    for cp in sends:
        cp.wait_recv()


def on_device(envelope, mode_profile, dispersion, kerr_gain):
    count = lax.axis_size("mode")
    peers = [(dy, dz, dc) for dy in range(4) for dz in range(4) for dc in range(2) if (dy, dz, dc) != (0, 0, 0)]
    peers.sort(key=lambda d: -(min(d[0], 4 - d[0]) + 2 * min(d[1], 4 - d[1])))
    n = len(peers)
    modes, grid = mode_profile.shape
    main, halo, pick = (jnp.asarray(c) for c in constants())
    hbm, vmem = pl.BlockSpec(memory_space=pl.ANY), pl.BlockSpec(memory_space=pltpu.VMEM)
    dma = pltpu.SemaphoreType.DMA
    back = pl.pallas_call(
        functools.partial(kernel, peers, count),
        out_shape=jax.ShapeDtypeStruct((count, 16, 2 * W), BF16),
        in_specs=[hbm, hbm, hbm, vmem, vmem, vmem, vmem],
        out_specs=hbm,
        scratch_shapes=[
            pltpu.VMEM(envelope.shape, BF16),
            pltpu.VMEM((modes, grid), BF16),
            pltpu.VMEM((grid, modes), BF16),
            pltpu.VMEM((modes, 2 * W), BF16),
            pltpu.VMEM((modes, 2 * W), BF16),
            pltpu.VMEM((modes, 2 * W), F32),
            pltpu.VMEM((modes, 2 * W), F32),
            pltpu.VMEM((count, 16, 2 * W), BF16),
            pltpu.VMEM((modes, 2 * W), BF16),
            pltpu.VMEM((2, 2, 16, modes), BF16),
            pltpu.VMEM((2, 2, 16, modes), BF16),
            pltpu.VMEM((3, 16), F32),
            pltpu.VMEM((8, W), F32),
            pltpu.VMEM((count, 1, W), F32),
            pltpu.VMEM((4, modes, W), F32),
            dma((4,)), dma((4,)), dma((n,)), dma((n,)), dma((n,)), dma((n,)),
            dma((2, 2)), dma((2, 2)), dma((n,)), dma((n,)),
        ],
        compiler_params=pltpu.CompilerParams(collective_id=1, has_side_effects=True, vmem_limit_bytes=60 * 2**20),
    )(envelope, mode_profile, dispersion, kerr_gain.reshape(4, W), main, halo, pick)
    added = back.reshape(count, 16, 2, W).transpose(1, 2, 0, 3).reshape(envelope.shape)
    return envelope.astype(F32) + added.astype(F32)


def solution(mesh):
    placed = (P("mode", None, "tm"), P(), P(None, "mode"), P())
    return jax.shard_map(
        on_device, mesh=mesh, in_specs=placed, out_specs=P("mode", None, "tm"), check_vma=False
    )
```

time: 175 us -> 46.9 us (0.27)
  matrix products: 54.6 us -> 0 us
  waiting for transfers between devices: 46.4 us -> 0 us
  Pallas kernels: 0 us -> 44.3 us
  starting transfers between devices: 36.1 us -> 0 us
  other arithmetic: 16.4 us -> 1.07 us
  local copies, waits for them, and re-layouts: 13.7 us -> 1.21 us
  loops' own time: 5.79 us -> 0 us
    dot_general x32 -> x0, matrix products: 54.6 us -> none  [the longest x16 27.3 us: accumulate(): lax.dot_general(profile_pair[which_pol], field_pair[which_pol], (((0,), (...]
    pallas_call x0 -> x1, Pallas kernels: none -> 44.3 us  [on_device(): pl.pallas_call(functools.partial(kernel, peers, count), out_shape=jax.Sha...]
    all_to_all x4 -> x0, waiting for transfers between devices: 42.3 us -> none  [the longest x2 31.2 us: kerr_round(): lax.all_to_all(remote, 'mode', split_axis=0, concat_axis=2, tiled=True)]
    all_to_all x4 -> x0, starting transfers between devices: 28.9 us -> none  [the longest x2 17.7 us: kerr_round(): lax.all_to_all(split_blocks(signal, count), 'mode', split_axis=2, concat_...]
    ppermute x4 -> x0, starting transfers between devices: 7.18 us -> none  [the longest x2 5.93 us: padded_2(): after = lax.ppermute(leading, axis, down)]
    another operation x2 -> x0, loops' own time: 5.79 us -> none  [kerr_terms(): lax.scan(accumulate, jnp.zeros((mode_count, 2 * columns), jnp.float32), j...]
    convert_element_type x11 -> x0, other arithmetic: 5.02 us -> none  [the longest x8 4.74 us: accumulate(): cubic_pair = [(intensity[:, None, :] * grid_field).astype(jnp.bfloat16).r...]
    reshape x6 -> x0, local copies, waits for them, and re-layouts: 4.77 us -> none  [the longest x2 2.58 us: split_blocks(): signal.reshape(signal.shape[0], signal.shape[1], count, signal.shape[2] /...]
  transfers between devices with their start and end apart: 8 -> 0, of which waited for: 6 -> 0; matrix products, arithmetic and copies ran while one was open for 5% -> 0% of each run, Pallas kernels for 0% -> 0%
where the time goes in v1:
time: 46.9 us; the launch traced here: 46.6 us
  Pallas kernels  44.3 us (94%)
  local copies, waits for them, and re-layouts  1.21 us (3%)
  other arithmetic  1.07 us (2%)
    pallas_call x1, Pallas kernels, on_device(): pl.pallas_call(functools.partial(kernel, peers, count), out_shape=jax.Sha...  44.3 us
    convert_element_type x1, local copies, waits for them, and re-layouts, on_device(): return envelope.astype(F32) + added.astype(F32)  1.21 us
    add x1, other arithmetic, on_device(): return envelope.astype(F32) + added.astype(F32)  1.07 us

profile of v1, /device:TPU:1, one launch (start us, length us, event | category | flops | bytes accessed | tf_op | source)
XLA Modules:
  0.0 46.6 jit_solution(12918632265429770702)
XLA Ops:
  0.0 0.0 copy-start
  0.0 44.3 %shard_map.73 = bf16[32,16,256]{2,1,0:T(8,128)(2,1)} custom-call(bf16[16,2,4096]{2,1,0:T(2,128)(2,1)} %env_ref.1, bf16[512,8192]{1,0:T(8,128)(2,1)} %prof_ref.1, f32[3,16]{1,0:T(4,128)} %disp_ref.1, f32[4,128]{1,0:T(4,128)} %bitcast.7, bf16[256,384]{1,0:T(8,128)(2,1)} %constant.6.clone.main_ref, bf16[64,768]{1,0:T(8,128)(2,1)} %constant.7.clone.halo_ref, ...), custom_call_target="tpu_custom_call" | custom-call | tf_op jit(solution)/shard_map/pallas_call | solution.py:230
  44.3 1.2 %reshape.11 = f32[32,16,2,128]{3,2,1,0:T(2,128)S(1)} reshape(bf16[32,16,256]{2,1,0:T(8,128)(2,1)} %shard_map.73) | data formatting | bytes 786432 | tf_op jit(solution)/shard_map/convert_element_type | solution.py:257
  45.5 0.0 copy-done
  45.5 1.1 %bitcast_add_fusion = f32[16,2,4096]{2,1,0:T(2,128)} fusion(bf16[16,2,4096]{2,1,0:T(2,128)(2,1)S(1)} %copy-done, f32[32,16,2,128]{3,2,1,0:T(2,128)S(1)} %reshape.11), kind=kLoop, calls=%fused_computation | loop fusion | flops 262144 | bytes 1310720 | tf_op jit(solution)/shard_map/add | solution.py:257
Async XLA Ops:
  0.0 45.5 %copy-start = (bf16[16,2,4096]{2,1,0:T(2,128)(2,1)S(1)}, bf16[16,2,4096]{2,1,0:T(2,128)(2,1)}, u32[]{:S(2)}) copy-start(bf16[16,2,4096]{2,1,0:T(2,128)(2,1)} %env_ref.1) | copy-start | bytes 786436

commit v2 on v1

v2 whole, which is shorter than its diff:
```python
import functools

import jax
import jax.numpy as jnp
import ml_dtypes
import numpy as np
from jax import lax
from jax.experimental import pallas as pl
from jax.experimental.pallas import tpu as pltpu
from jax.sharding import PartitionSpec as P

FIRST_DIFF = (1.0 / 280, -4.0 / 105, 1.0 / 5, -4.0 / 5, 0.0, 4.0 / 5, -1.0 / 5, 4.0 / 105, -1.0 / 280)
SECOND_DIFF = (-1.0 / 560, 8.0 / 315, -1.0 / 5, 8.0 / 5, -205.0 / 72, 8.0 / 5, -1.0 / 5, 8.0 / 315, -1.0 / 560)
THIRD_DIFF = (7.0 / 240, -3.0 / 10, 169.0 / 120, -61.0 / 30, 0.0, 61.0 / 30, -169.0 / 120, 3.0 / 10, -7.0 / 240)

MESH = pl.DeviceIdType.MESH
F32, BF16 = jnp.float32, jnp.bfloat16
NT = (((1,), (1,)), ((), ()))
TN = (((0,), (0,)), ((), ()))
W = 128


def hi_lo(x):
    hi = x.astype(ml_dtypes.bfloat16)
    lo = (x - hi.astype(np.float64)).astype(ml_dtypes.bfloat16)
    return hi, lo


def constants():
    taps = (np.array(FIRST_DIFF), np.array(SECOND_DIFF) / 2, np.array(THIRD_DIFF) / 6)
    main = np.zeros((W, 3 * W))
    halo = np.zeros((32, 6 * W))
    for which, tap in enumerate(taps):
        for t in range(W):
            for k in range(-4, 5):
                s, col = t + k, which * W + t
                if 0 <= s < W:
                    main[s, col] = tap[k + 4]
                else:
                    row = s + 4 if s < 0 else 16 + s - W
                    halo[row, col] = tap[k + 4]
                    halo[row + 4, 3 * W + col] = tap[k + 4]
    pick = np.zeros((32, 2 * W))
    for j in range(4):
        pick[j, j] = pick[4 + j, W + j] = 1
        pick[16 + j, W - 4 + j] = pick[20 + j, 2 * W - 4 + j] = 1
    return np.concatenate(hi_lo(main), 0), np.concatenate(hi_lo(halo), 0), pick.astype(ml_dtypes.bfloat16)


def dot(a, b, dims=(((1,), (0,)), ((), ()))):
    return lax.dot_general(a, b, dims, preferred_element_type=F32)


def place(y, z, c):
    z = z + (y % 2) * (3 - 2 * z)
    return y * 8 + z * 2 + (c + z) % 2


def device_at(pos):
    y, z = pos // 8, (pos // 2) % 4
    c = (pos % 2 + z) % 2
    z = z + (y % 2) * (3 - 2 * z)
    return y * 8 + z * 2 + c


def kernel(
    peers, count, env_ref, prof_ref, disp_ref, gain_ref, main_ref, halo_ref, pick_ref, back_ref,
    env, prof, proft, own_grid, cubic, field, mid, first, proj, sendbuf, incr, edges, halos, disp, drow, dall, coef, got,
    gain, main, halo, pick, lsem, psem, ssem, rsem, dssem, drsem, hssem, hrsem, bssem, brsem,
):
    me, tm = lax.axis_index("mode"), lax.axis_index("tm")
    slabs = lax.axis_size("tm")
    grid = prof.shape[1]
    parts = psem.shape[1]
    width = grid // parts
    y, z, c = me // 8, (me // 2) % 4, me % 2
    half = y // 2

    def to(peer):
        dy, dz, dc = peer
        py = (y, y + 1 - 2 * (y % 2), (y + 2) % 4, 3 - y)[dy]
        return py * 8 + ((z + dz) % 4) * 2 + (c + dc) % 2

    def back_from(peer):
        return to((peer[0], (4 - peer[1]) % 4, peer[2]))

    def rows(device, pol):
        return pl.ds(pl.multiple_of(((device + 16 * pol) % count) * 16, 16), 16)

    here = place(y, z, c)
    right = (device_at((here + 1) % count), (tm + (here + 1) // count) % slabs)
    left = (device_at((here + count - 1) % count), (tm + slabs - (count - here) // count) % slabs)

    barrier = pltpu.get_barrier_semaphore()
    for peer in peers:
        pl.semaphore_signal(barrier, inc=1, device_id=(to(peer), tm), device_id_type=MESH)
    for who in (left, right):
        pl.semaphore_signal(barrier, inc=1, device_id=who, device_id_type=MESH)

    loads = [
        pltpu.make_async_copy(a, b, lsem.at[i])
        for i, (a, b) in enumerate(
            ((env_ref, env), (disp_ref, disp), (gain_ref, gain), (pick_ref, pick), (main_ref, main), (halo_ref, halo))
        )
    ]
    for cp in loads:
        cp.start()

    def prof_in(i, q):
        cols = pl.ds(i * width, width)
        pol = pl.ds(pl.multiple_of(256 * ((half + q) % 2), 256), 256)
        return pltpu.make_async_copy(prof_ref.at[pol, cols], prof.at[256 * q : 256 * q + 256, cols], psem.at[q, i])

    for i in range(parts):
        for q in (0, 1):
            prof_in(i, q).start()

    loads[0].wait()
    for p in range(count):
        k = place(p // 8, (p // 2) % 4, p % 2)
        block = env[:, :, k * W : (k + 1) * W]
        sendbuf[p, :, 0:W] = block[:, 0, :]
        sendbuf[p, :, W : 2 * W] = block[:, 1, :]
    loads[1].wait()
    drow[...] = jnp.zeros_like(drow)
    drow[0:3, 0:16] = disp[...]
    lines = drow[...]
    drow[0:1, :] = lines[0:1] + pltpu.roll(lines[1:2], 16, 1) + pltpu.roll(lines[2:3], 32, 1)
    dall[me % 16] = drow[0:1, :]

    pl.semaphore_wait(barrier, len(peers) + 2)

    own = pltpu.make_async_copy(sendbuf.at[me], field.at[rows(me, half), :], lsem.at[6])
    own.start()
    sends, dsends = [], []
    for j, peer in enumerate(peers):
        other = to(peer)
        sends.append(pltpu.make_async_remote_copy(
            src_ref=sendbuf.at[other], dst_ref=field.at[rows(me, half if peer[0] < 2 else 1 - half), :],
            send_sem=ssem.at[j], recv_sem=rsem.at[j], device_id=(other, tm), device_id_type=MESH))
        sends[-1].start()

    unit = (lax.broadcasted_iota(jnp.int32, (256, 256), 0) == lax.broadcasted_iota(jnp.int32, (256, 256), 1)).astype(BF16)
    for i in range(parts):
        for q in (0, 1):
            prof_in(i, q).wait()

        def flip(b, _, i=i):
            at = pl.ds(pl.multiple_of(i * width + b * 256, 256), 256)
            for q in (0, 1):
                proft[at, 256 * q : 256 * q + 256] = dot(unit, prof[256 * q : 256 * q + 256, at], NT).astype(BF16)
            return 0

        lax.fori_loop(0, width // 256, flip, 0, unroll=True)

    for j, peer in enumerate(peers):
        slot = (me + 16 * (half if peer[0] < 2 else 1 - half)) % count
        dsends.append(pltpu.make_async_remote_copy(
            src_ref=drow.at[0:1], dst_ref=dall.at[slot], send_sem=dssem.at[j], recv_sem=drsem.at[j],
            device_id=(to(peer), tm), device_id_type=MESH))
        dsends[-1].start()

    loads[2].wait()
    diagonal = lax.broadcasted_iota(jnp.int32, (W, W), 0) == lax.broadcasted_iota(jnp.int32, (W, W), 1)
    for r in range(4):
        picked = jnp.where(diagonal, gain[pl.ds((r + 2 * half) % 4, 1), :] * (256.0 / grid), 0.0)
        coef[3, r * W : (r + 1) * W, :] = jnp.broadcast_to(jnp.sum(picked, 1, keepdims=True), (W, W))

    for cp in loads[3:]:
        cp.wait()

    def grid_field(src, q, at):
        return dot(proft[at, 256 * q : 256 * q + 256], src[256 * q : 256 * q + 256, :])

    step = 2048
    blocks = [slice(b * step, (b + 1) * step) for b in range(grid // step)]

    own.wait()
    for cp, peer in zip(sends, peers):
        if peer[0] < 2:
            cp.wait_recv()
    for at in blocks:
        own_grid[at, :] = grid_field(field, 0, at)
    for cp, peer in zip(sends, peers):
        if peer[0] >= 2:
            cp.wait_recv()

    def send_edges(values, turn):
        edges[turn] = dot(pick[...], values, NT).astype(BF16).reshape(2, 16, 512)
        out = []
        for side, who in ((0, left), (1, right)):
            out.append(pltpu.make_async_remote_copy(
                src_ref=edges.at[turn, side], dst_ref=halos.at[turn, 1 - side], send_sem=hssem.at[turn, side],
                recv_sem=hrsem.at[turn, 1 - side], device_id=who, device_id_type=MESH))
            out[-1].start()
        return out

    hsends = send_edges(field[...], 0)
    for cp in dsends:
        cp.wait_recv()
    lane, sub = (lax.broadcasted_iota(jnp.int32, (16, W), d) for d in (1, 0))
    for i in range(count):
        row = jnp.broadcast_to(dall[i], (16, W))
        for d in range(3):
            column = jnp.sum(jnp.where(lane == sub + 16 * d, row, 0.0), 1, keepdims=True)
            coef[d, 16 * i : 16 * i + 16, :] = jnp.broadcast_to(column, (16, W))

    def cube(g):
        level = g[0][:, :W] ** 2 + g[0][:, W:] ** 2 + g[1][:, :W] ** 2 + g[1][:, W:] ** 2
        level = jnp.concatenate([level, level], 1)
        return [(level * part).astype(BF16) for part in g]

    def linear(src, turn, q):
        at = slice(256 * q, 256 * q + 256)
        values = src[at, :]
        re, im = values[:, :W], values[:, W:]
        ends = [
            halos[turn, s, :, pl.ds(pl.multiple_of(256 * ((q + half + who[0] // 16) % 2), 256), 256)]
            for s, who in ((0, left), (1, right))
        ]
        side = jnp.concatenate(ends, 0).astype(F32).T.astype(BF16)
        side = dot(jnp.concatenate([side, side], 1), halo[...])
        d_re = dot(jnp.concatenate([re, re], 1), main[...]) + side[:, : 3 * W]
        d_im = dot(jnp.concatenate([im, im], 1), main[...]) + side[:, 3 * W :]
        walk, spread, skew = (coef[d, at, :] for d in range(3))
        out_re = skew * d_re[:, 2 * W :] - walk * d_re[:, :W] + spread * d_im[:, W : 2 * W]
        out_im = skew * d_im[:, 2 * W :] - walk * d_im[:, :W] - spread * d_re[:, W : 2 * W]
        return jnp.concatenate([out_re, out_im], 1)

    def turned(values, q):
        scale = coef[3, 256 * q : 256 * q + 256, :]
        return jnp.concatenate([-scale * values[:, W:], scale * values[:, :W]], 1)

    for b, at in enumerate(blocks):
        parts_ = cube([own_grid[at, :], grid_field(field, 1, at)])
        for q in (0, 1):
            part = dot(prof[256 * q : 256 * q + 256, at], parts_[q])
            if b == 0:
                proj[256 * q : 256 * q + 256, :] = part
            else:
                proj[256 * q : 256 * q + 256, :] += part
    for cp in hsends:
        cp.wait_recv()
    for q in (0, 1):
        at = slice(256 * q, 256 * q + 256)
        rate = linear(field, 0, q) + turned(proj[at, :], q)
        first[at, :] = rate
        mid[at, :] = (field[at, :].astype(F32) + rate).astype(BF16)
    hsends += send_edges(mid[...], 1)

    for at in blocks:
        parts_ = cube([grid_field(mid, q, at) for q in (0, 1)])
        for q in (0, 1):
            cubic[q, at, :] = parts_[q]
    for cp in hsends[2:]:
        cp.wait_recv()
    returns = {}
    for q in (1, 0):
        at = slice(256 * q, 256 * q + 256)
        known = first[at, :] + linear(mid, 1, q)
        proj[at, :] = dot(prof[at, :], cubic[q])
        incr[at, :] = (0.5 * (known + turned(proj[at, :], q))).astype(BF16)
        for j, peer in enumerate(peers):
            if (peer[0] >= 2) == (q == 1):
                other = to(peer)
                returns[j] = pltpu.make_async_remote_copy(
                    src_ref=incr.at[rows(other, half), :], dst_ref=got.at[me], send_sem=bssem.at[j],
                    recv_sem=brsem.at[j], device_id=(other, tm), device_id_type=MESH)
                returns[j].start()
    own = pltpu.make_async_copy(incr.at[rows(me, half), :], got.at[me], lsem.at[7])
    own.start()

    def hand_on(source):
        k = place(source // 8, (source // 2) % 4, source % 2)
        values = got[source].astype(F32)
        pair = jnp.stack([values[:, :W], values[:, W:]], 1).astype(BF16)
        back_ref[:, :, pl.ds(pl.multiple_of(k * W, W), W)] = pair

    own.wait()
    hand_on(me)
    for near in range(n_far(peers)):
        for j, peer in enumerate(peers):
            if distance(peer) == near:
                returns[j].wait_recv()
                hand_on(back_from(peer))
    for cp in [*sends, *dsends, *hsends, *returns.values()]:
        cp.wait_send()


def distance(peer):
    dy, dz, dc = peer
    return min(dz, 4 - dz) + 4 * (dy // 2)


def n_far(peers):
    return 1 + max(distance(p) for p in peers)


def on_device(envelope, mode_profile, dispersion, kerr_gain):
    count = lax.axis_size("mode")
    peers = [(dy, dz, dc) for dy in range(4) for dz in (2, 1, 3, 0) for dc in range(2) if (dy, dz, dc) != (0, 0, 0)]
    peers.sort(key=lambda d: (d[0] // 2, -min(d[1], 4 - d[1])))
    n = len(peers)
    modes, grid = mode_profile.shape
    consts = [jnp.asarray(c) for c in constants()]
    hbm, vmem = pl.BlockSpec(memory_space=pl.ANY), pl.BlockSpec(memory_space=pltpu.VMEM)
    dma = pltpu.SemaphoreType.DMA
    added = pl.pallas_call(
        functools.partial(kernel, peers, count),
        out_shape=jax.ShapeDtypeStruct(envelope.shape, BF16),
        in_specs=[hbm] * 7,
        out_specs=vmem,
        scratch_shapes=[
            pltpu.VMEM(envelope.shape, BF16),
            pltpu.VMEM((modes, grid), BF16),
            pltpu.VMEM((grid, modes), BF16),
            pltpu.VMEM((grid, 2 * W), F32),
            pltpu.VMEM((2, grid, 2 * W), BF16),
            pltpu.VMEM((modes, 2 * W), BF16),
            pltpu.VMEM((modes, 2 * W), BF16),
            pltpu.VMEM((modes, 2 * W), F32),
            pltpu.VMEM((modes, 2 * W), F32),
            pltpu.VMEM((count, 16, 2 * W), BF16),
            pltpu.VMEM((modes, 2 * W), BF16),
            pltpu.VMEM((2, 2, 16, modes), BF16),
            pltpu.VMEM((2, 2, 16, modes), BF16),
            pltpu.VMEM((3, 16), F32),
            pltpu.VMEM((8, W), F32),
            pltpu.VMEM((count, 1, W), F32),
            pltpu.VMEM((4, modes, W), F32),
            pltpu.VMEM((count, 16, 2 * W), BF16),
            pltpu.VMEM((4, W), F32),
            *[pltpu.VMEM(c.shape, BF16) for c in consts],
            dma((8,)), dma((2, 4)), dma((n,)), dma((n,)), dma((n,)), dma((n,)),
            dma((2, 2)), dma((2, 2)), dma((n,)), dma((n,)),
        ],
        compiler_params=pltpu.CompilerParams(collective_id=1, has_side_effects=True, vmem_limit_bytes=60 * 2**20),
    )(envelope, mode_profile, dispersion, kerr_gain.reshape(4, W), *consts)
    return envelope.astype(F32) + added.astype(F32)


def solution(mesh):
    placed = (P("mode", None, "tm"), P(), P(None, "mode"), P())
    return jax.shard_map(
        on_device, mesh=mesh, in_specs=placed, out_specs=P("mode", None, "tm"), check_vma=False
    )
```

time: 46.9 us -> 47.7 us (1.017)
  Pallas kernels: 44.3 us -> 45.8 us
  local copies, waits for them, and re-layouts: 1.21 us -> 0.01 us
  other arithmetic: 1.07 us -> 1.8 us
    pallas_call x1, Pallas kernels: 44.3 us -> 45.8 us  [on_device(): pl.pallas_call(functools.partial(kernel, peers, count), out_shape=jax.Sha...]
    convert_element_type x1 -> x0, local copies, waits for them, and re-layouts: 1.21 us -> none  [on_device(): return envelope.astype(F32) + added.astype(F32)]
    add x1, other arithmetic: 1.07 us -> 1.8 us  [on_device(): return envelope.astype(F32) + added.astype(F32)]
where the time goes in v2:
time: 47.7 us; the launch traced here: 47.6 us
  Pallas kernels  45.8 us (96%)
  other arithmetic  1.8 us (4%)
    pallas_call x1, Pallas kernels, on_device(): pl.pallas_call(functools.partial(kernel, peers, count), out_shape=jax.Sha...  45.8 us
    add x1, other arithmetic, on_device(): return envelope.astype(F32) + added.astype(F32)  1.8 us

profile of v2, /device:TPU:1, one launch (start us, length us, event | category | flops | bytes accessed | tf_op | source)
XLA Modules:
  0.0 47.6 jit_solution(10507081629215977288)
XLA Ops:
  0.0 0.0 copy-start
  0.0 45.8 %shard_map.73 = bf16[16,2,4096]{2,1,0:T(2,128)(2,1)} custom-call(bf16[16,2,4096]{2,1,0:T(2,128)(2,1)} %env_ref.1, bf16[512,8192]{1,0:T(8,128)(2,1)} %prof_ref.1, f32[3,16]{1,0:T(4,128)} %disp_ref.1, f32[4,128]{1,0:T(4,128)} %bitcast.6, bf16[256,384]{1,0:T(8,128)(2,1)} %constant.6.clone.main_ref, bf16[64,768]{1,0:T(8,128)(2,1)} %constant.7.clone.halo_ref, ...), custom_call_target="tpu_custom_call" | custom-call | tf_op jit(solution)/shard_map/pallas_call | solution.py:308
  45.8 0.0 copy-done
  45.8 1.8 %convert_add_fusion = f32[4,8,4096]{2,1,0:T(8,128)} fusion(bf16[4,8,4096]{2,1,0:T(8,128)(2,1)} %bitcast.5, bf16[4,8,4096]{2,1,0:T(8,128)(2,1)S(1)} %bitcast.4), kind=kLoop, calls=%fused_computation | loop fusion | flops 393216 | bytes 1048576 | tf_op jit(solution)/shard_map/add | solution.py:339
Async XLA Ops:
  0.0 45.8 %copy-start = (bf16[16,2,4096]{2,1,0:T(2,128)(2,1)S(1)}, bf16[16,2,4096]{2,1,0:T(2,128)(2,1)}, u32[]{:S(2)}) copy-start(bf16[16,2,4096]{2,1,0:T(2,128)(2,1)} %env_ref.1) | copy-start | bytes 786436

commit v3 on v2

--- a/solution.py
+++ b/solution.py
@@ -64,7 +64,7 @@
 
 
 def kernel(
-    peers, count, env_ref, prof_ref, disp_ref, gain_ref, main_ref, halo_ref, pick_ref, back_ref,
+    peers, count, env_ref, prof_ref, disp_ref, gain_ref, main_ref, halo_ref, pick_ref, out_ref,
     env, prof, proft, own_grid, cubic, field, mid, first, proj, sendbuf, incr, edges, halos, disp, drow, dall, coef, got,
     gain, main, halo, pick, lsem, psem, ssem, rsem, dssem, drsem, hssem, hrsem, bssem, brsem,
 ):
@@ -210,18 +210,24 @@
         level = jnp.concatenate([level, level], 1)
         return [(level * part).astype(BF16) for part in g]
 
-    def linear(src, turn, q):
+    def interior(src, q):
         at = slice(256 * q, 256 * q + 256)
         values = src[at, :]
         re, im = values[:, :W], values[:, W:]
+        d_re = dot(jnp.concatenate([re, re], 1), main[...])
+        d_im = dot(jnp.concatenate([im, im], 1), main[...])
+        return combined(d_re, d_im, at)
+
+    def fringe(turn, q):
         ends = [
             halos[turn, s, :, pl.ds(pl.multiple_of(256 * ((q + half + who[0] // 16) % 2), 256), 256)]
             for s, who in ((0, left), (1, right))
         ]
         side = jnp.concatenate(ends, 0).astype(F32).T.astype(BF16)
         side = dot(jnp.concatenate([side, side], 1), halo[...])
-        d_re = dot(jnp.concatenate([re, re], 1), main[...]) + side[:, : 3 * W]
-        d_im = dot(jnp.concatenate([im, im], 1), main[...]) + side[:, 3 * W :]
+        return combined(side[:, : 3 * W], side[:, 3 * W :], slice(256 * q, 256 * q + 256))
+
+    def combined(d_re, d_im, at):
         walk, spread, skew = (coef[d, at, :] for d in range(3))
         out_re = skew * d_re[:, 2 * W :] - walk * d_re[:, :W] + spread * d_im[:, W : 2 * W]
         out_im = skew * d_im[:, 2 * W :] - walk * d_im[:, :W] - spread * d_re[:, W : 2 * W]
@@ -231,6 +237,8 @@
         scale = coef[3, 256 * q : 256 * q + 256, :]
         return jnp.concatenate([-scale * values[:, W:], scale * values[:, :W]], 1)
 
+    for q in (0, 1):
+        first[256 * q : 256 * q + 256, :] = interior(field, q)
     for b, at in enumerate(blocks):
         parts_ = cube([own_grid[at, :], grid_field(field, 1, at)])
         for q in (0, 1):
@@ -243,23 +251,25 @@
         cp.wait_recv()
     for q in (0, 1):
         at = slice(256 * q, 256 * q + 256)
-        rate = linear(field, 0, q) + turned(proj[at, :], q)
+        rate = first[at, :] + fringe(0, q) + turned(proj[at, :], q)
         first[at, :] = rate
         mid[at, :] = (field[at, :].astype(F32) + rate).astype(BF16)
     hsends += send_edges(mid[...], 1)
 
+    for q in (0, 1):
+        first[256 * q : 256 * q + 256, :] += interior(mid, q)
     for at in blocks:
         parts_ = cube([grid_field(mid, q, at) for q in (0, 1)])
         for q in (0, 1):
             cubic[q, at, :] = parts_[q]
-    for cp in hsends[2:]:
-        cp.wait_recv()
     returns = {}
     for q in (1, 0):
         at = slice(256 * q, 256 * q + 256)
-        known = first[at, :] + linear(mid, 1, q)
         proj[at, :] = dot(prof[at, :], cubic[q])
-        incr[at, :] = (0.5 * (known + turned(proj[at, :], q))).astype(BF16)
+        if q == 1:
+            for cp in hsends[2:]:
+                cp.wait_recv()
+        incr[at, :] = (0.5 * (first[at, :] + fringe(1, q) + turned(proj[at, :], q))).astype(BF16)
         for j, peer in enumerate(peers):
             if (peer[0] >= 2) == (q == 1):
                 other = to(peer)
@@ -273,8 +283,9 @@
     def hand_on(source):
         k = place(source // 8, (source // 2) % 4, source % 2)
         values = got[source].astype(F32)
-        pair = jnp.stack([values[:, :W], values[:, W:]], 1).astype(BF16)
-        back_ref[:, :, pl.ds(pl.multiple_of(k * W, W), W)] = pair
+        pair = jnp.stack([values[:, :W], values[:, W:]], 1)
+        at = pl.ds(pl.multiple_of(k * W, W), W)
+        out_ref[:, :, at] = env[:, :, at].astype(F32) + pair
 
     own.wait()
     hand_on(me)
@@ -305,9 +316,9 @@
     consts = [jnp.asarray(c) for c in constants()]
     hbm, vmem = pl.BlockSpec(memory_space=pl.ANY), pl.BlockSpec(memory_space=pltpu.VMEM)
     dma = pltpu.SemaphoreType.DMA
-    added = pl.pallas_call(
+    return pl.pallas_call(
         functools.partial(kernel, peers, count),
-        out_shape=jax.ShapeDtypeStruct(envelope.shape, BF16),
+        out_shape=pltpu.VMEM(envelope.shape, F32),
         in_specs=[hbm] * 7,
         out_specs=vmem,
         scratch_shapes=[
@@ -336,7 +347,6 @@
         ],
         compiler_params=pltpu.CompilerParams(collective_id=1, has_side_effects=True, vmem_limit_bytes=60 * 2**20),
     )(envelope, mode_profile, dispersion, kerr_gain.reshape(4, W), *consts)
-    return envelope.astype(F32) + added.astype(F32)
 
 
 def solution(mesh):

time: 47.7 us -> 43.9 us (0.920)
  Pallas kernels: 45.8 us -> 43.1 us
  other arithmetic: 1.8 us -> 0 us
  local copies, waits for them, and re-layouts: 0.01 us -> 0.8 us
    pallas_call x1, Pallas kernels: 45.8 us -> 43.1 us  [on_device(): pl.pallas_call(functools.partial(kernel, peers, count), out_shape=pltpu.V...]
    add x1 -> x0, other arithmetic: 1.8 us -> none  [on_device(): return envelope.astype(F32) + added.astype(F32)]
    unnamed x2 -> x1, local copies, waits for them, and re-layouts: 0.01 us -> 0.8 us
where the time goes in v3:
time: 43.9 us
  Pallas kernels  43.1 us (98%)
  local copies, waits for them, and re-layouts  0.8 us (2%)
    pallas_call x1, Pallas kernels, on_device(): pl.pallas_call(functools.partial(kernel, peers, count), out_shape=pltpu.V...  43.1 us

profile of v3, /device:TPU:1, one launch (start us, length us, event | category | flops | bytes accessed | tf_op | source)
XLA Modules:
  0.0 43.9 jit_solution(4985558515478403789)
XLA Ops:
  0.0 43.1 %shard_map.73 = f32[16,2,4096]{2,1,0:T(2,128)S(1)} custom-call(bf16[16,2,4096]{2,1,0:T(2,128)(2,1)} %env_ref.1, bf16[512,8192]{1,0:T(8,128)(2,1)} %prof_ref.1, f32[3,16]{1,0:T(4,128)} %disp_ref.1, f32[4,128]{1,0:T(4,128)} %bitcast.1, bf16[256,384]{1,0:T(8,128)(2,1)} %constant.6.clone.main_ref, bf16[64,768]{1,0:T(8,128)(2,1)} %constant.7.clone.halo_ref, ...), custom_call_target="tpu_custom_call" | custom-call | tf_op jit(solution)/shard_map/pallas_call | solution.py:319
  43.1 0.8 %copy.9 = f32[16,2,4096]{2,1,0:T(2,128)} copy(f32[16,2,4096]{2,1,0:T(2,128)S(1)} %shard_map.73) | data formatting | bytes 1048576

commit v4 on v3

--- a/solution.py
+++ b/solution.py
@@ -74,25 +74,27 @@
     parts = psem.shape[1]
     width = grid // parts
     y, z, c = me // 8, (me // 2) % 4, me % 2
-    half = y // 2
+    turns = (y, y + 1 - 2 * (y % 2), (y + 2) % 4, 3 - y)
 
     def to(peer):
         dy, dz, dc = peer
-        py = (y, y + 1 - 2 * (y % 2), (y + 2) % 4, 3 - y)[dy]
-        return py * 8 + ((z + dz) % 4) * 2 + (c + dc) % 2
+        return turns[dy] * 8 + ((z + dz) % 4) * 2 + (c + dc) % 2
 
     def back_from(peer):
         return to((peer[0], (4 - peer[1]) % 4, peer[2]))
 
-    def rows(device, pol):
-        return pl.ds(pl.multiple_of(((device + 16 * pol) % count) * 16, 16), 16)
+    def slot(dy, device):
+        return dy * 8 + device % 8
+
+    def rows(dy, device):
+        return pl.ds(pl.multiple_of(slot(dy, device) * 16, 16), 16)
 
     here = place(y, z, c)
     right = (device_at((here + 1) % count), (tm + (here + 1) // count) % slabs)
     left = (device_at((here + count - 1) % count), (tm + slabs - (count - here) // count) % slabs)
 
     barrier = pltpu.get_barrier_semaphore()
-    for peer in peers:
+    for peer in sorted(peers, key=lambda d: -min(d[1], 4 - d[1])):
         pl.semaphore_signal(barrier, inc=1, device_id=(to(peer), tm), device_id_type=MESH)
     for who in (left, right):
         pl.semaphore_signal(barrier, inc=1, device_id=who, device_id_type=MESH)
@@ -108,11 +110,11 @@
 
     def prof_in(i, q):
         cols = pl.ds(i * width, width)
-        pol = pl.ds(pl.multiple_of(256 * ((half + q) % 2), 256), 256)
-        return pltpu.make_async_copy(prof_ref.at[pol, cols], prof.at[256 * q : 256 * q + 256, cols], psem.at[q, i])
+        fields = pl.ds(pl.multiple_of(W * turns[q], W), W)
+        return pltpu.make_async_copy(prof_ref.at[fields, cols], prof.at[W * q : W * q + W, cols], psem.at[q, i])
 
     for i in range(parts):
-        for q in (0, 1):
+        for q in range(4):
             prof_in(i, q).start()
 
     loads[0].wait()
@@ -126,23 +128,23 @@
     drow[0:3, 0:16] = disp[...]
     lines = drow[...]
     drow[0:1, :] = lines[0:1] + pltpu.roll(lines[1:2], 16, 1) + pltpu.roll(lines[2:3], 32, 1)
-    dall[me % 16] = drow[0:1, :]
+    dall[me % 8] = drow[0:1, :]
 
     pl.semaphore_wait(barrier, len(peers) + 2)
 
-    own = pltpu.make_async_copy(sendbuf.at[me], field.at[rows(me, half), :], lsem.at[6])
+    own = pltpu.make_async_copy(sendbuf.at[me], field.at[rows(0, me), :], lsem.at[6])
     own.start()
     sends, dsends = [], []
     for j, peer in enumerate(peers):
         other = to(peer)
         sends.append(pltpu.make_async_remote_copy(
-            src_ref=sendbuf.at[other], dst_ref=field.at[rows(me, half if peer[0] < 2 else 1 - half), :],
+            src_ref=sendbuf.at[other], dst_ref=field.at[rows(peer[0], me), :],
             send_sem=ssem.at[j], recv_sem=rsem.at[j], device_id=(other, tm), device_id_type=MESH))
         sends[-1].start()
 
     unit = (lax.broadcasted_iota(jnp.int32, (256, 256), 0) == lax.broadcasted_iota(jnp.int32, (256, 256), 1)).astype(BF16)
     for i in range(parts):
-        for q in (0, 1):
+        for q in range(4):
             prof_in(i, q).wait()
 
         def flip(b, _, i=i):
@@ -154,16 +156,15 @@
         lax.fori_loop(0, width // 256, flip, 0, unroll=True)
 
     for j, peer in enumerate(peers):
-        slot = (me + 16 * (half if peer[0] < 2 else 1 - half)) % count
         dsends.append(pltpu.make_async_remote_copy(
-            src_ref=drow.at[0:1], dst_ref=dall.at[slot], send_sem=dssem.at[j], recv_sem=drsem.at[j],
+            src_ref=drow.at[0:1], dst_ref=dall.at[slot(peer[0], me)], send_sem=dssem.at[j], recv_sem=drsem.at[j],
             device_id=(to(peer), tm), device_id_type=MESH))
         dsends[-1].start()
 
     loads[2].wait()
     diagonal = lax.broadcasted_iota(jnp.int32, (W, W), 0) == lax.broadcasted_iota(jnp.int32, (W, W), 1)
     for r in range(4):
-        picked = jnp.where(diagonal, gain[pl.ds((r + 2 * half) % 4, 1), :] * (256.0 / grid), 0.0)
+        picked = jnp.where(diagonal, gain[pl.ds(turns[r], 1), :] * (256.0 / grid), 0.0)
         coef[3, r * W : (r + 1) * W, :] = jnp.broadcast_to(jnp.sum(picked, 1, keepdims=True), (W, W))
 
     for cp in loads[3:]:
@@ -179,14 +180,20 @@
     for cp, peer in zip(sends, peers):
         if peer[0] < 2:
             cp.wait_recv()
-    for at in blocks:
-        own_grid[at, :] = grid_field(field, 0, at)
-    for cp, peer in zip(sends, peers):
-        if peer[0] >= 2:
-            cp.wait_recv()
-
-    def send_edges(values, turn):
-        edges[turn] = dot(pick[...], values, NT).astype(BF16).reshape(2, 16, 512)
+
+    def coefficients(q):
+        lane, sub = (lax.broadcasted_iota(jnp.int32, (16, W), d) for d in (1, 0))
+        for i in range(16 * q, 16 * q + 16):
+            row = jnp.broadcast_to(dall[i], (16, W))
+            for d in range(3):
+                column = jnp.sum(jnp.where(lane == sub + 16 * d, row, 0.0), 1, keepdims=True)
+                coef[d, 16 * i : 16 * i + 16, :] = jnp.broadcast_to(column, (16, W))
+
+    def form_edges(src, turn, q):
+        at = slice(256 * q, 256 * q + 256)
+        edges[turn, :, :, at] = dot(pick[...], src[at, :], NT).astype(BF16).reshape(2, 16, 256)
+
+    def send_edges(turn):
         out = []
         for side, who in ((0, left), (1, right)):
             out.append(pltpu.make_async_remote_copy(
@@ -195,16 +202,6 @@
             out[-1].start()
         return out
 
-    hsends = send_edges(field[...], 0)
-    for cp in dsends:
-        cp.wait_recv()
-    lane, sub = (lax.broadcasted_iota(jnp.int32, (16, W), d) for d in (1, 0))
-    for i in range(count):
-        row = jnp.broadcast_to(dall[i], (16, W))
-        for d in range(3):
-            column = jnp.sum(jnp.where(lane == sub + 16 * d, row, 0.0), 1, keepdims=True)
-            coef[d, 16 * i : 16 * i + 16, :] = jnp.broadcast_to(column, (16, W))
-
     def cube(g):
         level = g[0][:, :W] ** 2 + g[0][:, W:] ** 2 + g[1][:, :W] ** 2 + g[1][:, W:] ** 2
         level = jnp.concatenate([level, level], 1)
@@ -218,9 +215,13 @@
         d_im = dot(jnp.concatenate([im, im], 1), main[...])
         return combined(d_re, d_im, at)
 
+    def column(sender, d):
+        row = turns[d]
+        return pl.multiple_of(W * (2 * ((sender // 2 + row // 2) % 2) + (sender + row) % 2), W)
+
     def fringe(turn, q):
         ends = [
-            halos[turn, s, :, pl.ds(pl.multiple_of(256 * ((q + half + who[0] // 16) % 2), 256), 256)]
+            jnp.concatenate([halos[turn, s, :, pl.ds(column(who[0] // 8, d), W)] for d in (2 * q, 2 * q + 1)], 1)
             for s, who in ((0, left), (1, right))
         ]
         side = jnp.concatenate(ends, 0).astype(F32).T.astype(BF16)
@@ -233,13 +234,33 @@
         out_im = skew * d_im[:, 2 * W :] - walk * d_im[:, :W] - spread * d_re[:, W : 2 * W]
         return jnp.concatenate([out_re, out_im], 1)
 
-    def turned(values, q):
-        scale = coef[3, 256 * q : 256 * q + 256, :]
+    def turned(values, at):
+        scale = coef[3, at, :]
         return jnp.concatenate([-scale * values[:, W:], scale * values[:, :W]], 1)
 
-    for q in (0, 1):
-        first[256 * q : 256 * q + 256, :] = interior(field, q)
+    def arrived(copies, q):
+        for cp, peer in zip(copies, peers):
+            if peer[0] // 2 == q:
+                cp.wait_recv()
+
+    form_edges(field, 0, 0)
+    for at in blocks:
+        own_grid[at, :] = grid_field(field, 0, at)
+    arrived(dsends, 0)
+    coefficients(0)
+    first[0:256, :] = interior(field, 0)
+    arrived(sends, 1)
+    form_edges(field, 0, 1)
+    hsends = send_edges(0)
+    arrived(dsends, 1)
+    coefficients(1)
+    first[256:512, :] = interior(field, 1)
     for b, at in enumerate(blocks):
+        if b == len(blocks) - 1:
+            for cp in hsends:
+                cp.wait_recv()
+            for q in (0, 1):
+                first[256 * q : 256 * q + 256, :] += fringe(0, q)
         parts_ = cube([own_grid[at, :], grid_field(field, 1, at)])
         for q in (0, 1):
             part = dot(prof[256 * q : 256 * q + 256, at], parts_[q])
@@ -247,14 +268,13 @@
                 proj[256 * q : 256 * q + 256, :] = part
             else:
                 proj[256 * q : 256 * q + 256, :] += part
-    for cp in hsends:
-        cp.wait_recv()
     for q in (0, 1):
         at = slice(256 * q, 256 * q + 256)
-        rate = first[at, :] + fringe(0, q) + turned(proj[at, :], q)
+        rate = first[at, :] + turned(proj[at, :], at)
         first[at, :] = rate
         mid[at, :] = (field[at, :].astype(F32) + rate).astype(BF16)
-    hsends += send_edges(mid[...], 1)
+        form_edges(mid, 1, q)
+    hsends += send_edges(1)
 
     for q in (0, 1):
         first[256 * q : 256 * q + 256, :] += interior(mid, q)
@@ -263,21 +283,24 @@
         for q in (0, 1):
             cubic[q, at, :] = parts_[q]
     returns = {}
-    for q in (1, 0):
-        at = slice(256 * q, 256 * q + 256)
-        proj[at, :] = dot(prof[at, :], cubic[q])
-        if q == 1:
+    for group in (2, 3, 1, 0):
+        at = slice(W * group, W * group + W)
+        proj[at, :] = dot(prof[at, :], cubic[group // 2])
+        if group == 2:
             for cp in hsends[2:]:
                 cp.wait_recv()
-        incr[at, :] = (0.5 * (first[at, :] + fringe(1, q) + turned(proj[at, :], q))).astype(BF16)
+            first[256:512, :] += fringe(1, 1)
+        if group == 3:
+            first[0:256, :] += fringe(1, 0)
+        incr[at, :] = (0.5 * (first[at, :] + turned(proj[at, :], at))).astype(BF16)
         for j, peer in enumerate(peers):
-            if (peer[0] >= 2) == (q == 1):
+            if peer[0] == group:
                 other = to(peer)
                 returns[j] = pltpu.make_async_remote_copy(
-                    src_ref=incr.at[rows(other, half), :], dst_ref=got.at[me], send_sem=bssem.at[j],
+                    src_ref=incr.at[rows(group, other), :], dst_ref=got.at[me], send_sem=bssem.at[j],
                     recv_sem=brsem.at[j], device_id=(other, tm), device_id_type=MESH)
                 returns[j].start()
-    own = pltpu.make_async_copy(incr.at[rows(me, half), :], got.at[me], lsem.at[7])
+    own = pltpu.make_async_copy(incr.at[rows(0, me), :], got.at[me], lsem.at[7])
     own.start()
 
     def hand_on(source):
@@ -289,22 +312,15 @@
 
     own.wait()
     hand_on(me)
-    for near in range(n_far(peers)):
-        for j, peer in enumerate(peers):
-            if distance(peer) == near:
-                returns[j].wait_recv()
-                hand_on(back_from(peer))
+    for j in sorted(range(len(peers)), key=lambda j: ((2, 3, 1, 0).index(peers[j][0]), distance(peers[j]))):
+        returns[j].wait_recv()
+        hand_on(back_from(peers[j]))
     for cp in [*sends, *dsends, *hsends, *returns.values()]:
         cp.wait_send()
 
 
 def distance(peer):
-    dy, dz, dc = peer
-    return min(dz, 4 - dz) + 4 * (dy // 2)
-
-
-def n_far(peers):
-    return 1 + max(distance(p) for p in peers)
+    return min(peer[1], 4 - peer[1])
 
 
 def on_device(envelope, mode_profile, dispersion, kerr_gain):
@@ -342,7 +358,7 @@
             pltpu.VMEM((count, 16, 2 * W), BF16),
             pltpu.VMEM((4, W), F32),
             *[pltpu.VMEM(c.shape, BF16) for c in consts],
-            dma((8,)), dma((2, 4)), dma((n,)), dma((n,)), dma((n,)), dma((n,)),
+            dma((8,)), dma((4, 4)), dma((n,)), dma((n,)), dma((n,)), dma((n,)),
             dma((2, 2)), dma((2, 2)), dma((n,)), dma((n,)),
         ],
         compiler_params=pltpu.CompilerParams(collective_id=1, has_side_effects=True, vmem_limit_bytes=60 * 2**20),

time: 43.9 us -> 42.5 us (0.968)
  Pallas kernels: 43.1 us -> 41.6 us
    pallas_call x1, Pallas kernels: 43.1 us -> 41.6 us  [on_device(): pl.pallas_call(functools.partial(kernel, peers, count), out_shape=pltpu.V...]
where the time goes in v4:
time: 42.5 us; the launch traced here: 42.4 us
  Pallas kernels  41.6 us (98%)
  local copies, waits for them, and re-layouts  0.8 us (2%)
    pallas_call x1, Pallas kernels, on_device(): pl.pallas_call(functools.partial(kernel, peers, count), out_shape=pltpu.V...  41.6 us

profile of v4, /device:TPU:1, one launch (start us, length us, event | category | flops | bytes accessed | tf_op | source)
XLA Modules:
  0.0 42.4 jit_solution(8801517425427019135)
XLA Ops:
  0.0 41.6 %shard_map.73 = f32[16,2,4096]{2,1,0:T(2,128)S(1)} custom-call(bf16[16,2,4096]{2,1,0:T(2,128)(2,1)} %env_ref.1, bf16[512,8192]{1,0:T(8,128)(2,1)} %prof_ref.1, f32[3,16]{1,0:T(4,128)} %disp_ref.1, f32[4,128]{1,0:T(4,128)} %bitcast.1, bf16[256,384]{1,0:T(8,128)(2,1)} %constant.6.clone.main_ref, bf16[64,768]{1,0:T(8,128)(2,1)} %constant.7.clone.halo_ref, ...), custom_call_target="tpu_custom_call" | custom-call | tf_op jit(solution)/shard_map/pallas_call | solution.py:335
  41.6 0.8 %copy.9 = f32[16,2,4096]{2,1,0:T(2,128)} copy(f32[16,2,4096]{2,1,0:T(2,128)S(1)} %shard_map.73) | data formatting | bytes 1048576

commit v5 on v4

--- a/solution.py
+++ b/solution.py
@@ -113,10 +113,6 @@
         fields = pl.ds(pl.multiple_of(W * turns[q], W), W)
         return pltpu.make_async_copy(prof_ref.at[fields, cols], prof.at[W * q : W * q + W, cols], psem.at[q, i])
 
-    for i in range(parts):
-        for q in range(4):
-            prof_in(i, q).start()
-
     loads[0].wait()
     for p in range(count):
         k = place(p // 8, (p // 2) % 4, p % 2)
@@ -142,6 +138,15 @@
             send_sem=ssem.at[j], recv_sem=rsem.at[j], device_id=(other, tm), device_id_type=MESH))
         sends[-1].start()
 
+    for j, peer in enumerate(peers):
+        dsends.append(pltpu.make_async_remote_copy(
+            src_ref=drow.at[0:1], dst_ref=dall.at[slot(peer[0], me)], send_sem=dssem.at[j], recv_sem=drsem.at[j],
+            device_id=(to(peer), tm), device_id_type=MESH))
+        dsends[-1].start()
+    for i in range(parts):
+        for q in range(4):
+            prof_in(i, q).start()
+
     unit = (lax.broadcasted_iota(jnp.int32, (256, 256), 0) == lax.broadcasted_iota(jnp.int32, (256, 256), 1)).astype(BF16)
     for i in range(parts):
         for q in range(4):
@@ -154,12 +159,6 @@
             return 0
 
         lax.fori_loop(0, width // 256, flip, 0, unroll=True)
-
-    for j, peer in enumerate(peers):
-        dsends.append(pltpu.make_async_remote_copy(
-            src_ref=drow.at[0:1], dst_ref=dall.at[slot(peer[0], me)], send_sem=dssem.at[j], recv_sem=drsem.at[j],
-            device_id=(to(peer), tm), device_id_type=MESH))
-        dsends[-1].start()
 
     loads[2].wait()
     diagonal = lax.broadcasted_iota(jnp.int32, (W, W), 0) == lax.broadcasted_iota(jnp.int32, (W, W), 1)
@@ -256,11 +255,6 @@
     coefficients(1)
     first[256:512, :] = interior(field, 1)
     for b, at in enumerate(blocks):
-        if b == len(blocks) - 1:
-            for cp in hsends:
-                cp.wait_recv()
-            for q in (0, 1):
-                first[256 * q : 256 * q + 256, :] += fringe(0, q)
         parts_ = cube([own_grid[at, :], grid_field(field, 1, at)])
         for q in (0, 1):
             part = dot(prof[256 * q : 256 * q + 256, at], parts_[q])
@@ -268,9 +262,11 @@
                 proj[256 * q : 256 * q + 256, :] = part
             else:
                 proj[256 * q : 256 * q + 256, :] += part
+    for cp in hsends:
+        cp.wait_recv()
     for q in (0, 1):
         at = slice(256 * q, 256 * q + 256)
-        rate = first[at, :] + turned(proj[at, :], at)
+        rate = first[at, :] + fringe(0, q) + turned(proj[at, :], at)
         first[at, :] = rate
         mid[at, :] = (field[at, :].astype(F32) + rate).astype(BF16)
         form_edges(mid, 1, q)

time: 42.5 us -> 42.2 us (level)
  no operation moved by 1% of the time
where the time goes in v5:
time: 42.2 us
  Pallas kernels  41.3 us (98%)
  local copies, waits for them, and re-layouts  0.8 us (2%)
    pallas_call x1, Pallas kernels, on_device(): pl.pallas_call(functools.partial(kernel, peers, count), out_shape=pltpu.V...  41.3 us

profile of v5, /device:TPU:1, one launch (start us, length us, event | category | flops | bytes accessed | tf_op | source)
XLA Modules:
  0.0 42.2 jit_solution(9415990433620337763)
XLA Ops:
  0.0 41.3 %shard_map.73 = f32[16,2,4096]{2,1,0:T(2,128)S(1)} custom-call(bf16[16,2,4096]{2,1,0:T(2,128)(2,1)} %env_ref.1, bf16[512,8192]{1,0:T(8,128)(2,1)} %prof_ref.1, f32[3,16]{1,0:T(4,128)} %disp_ref.1, f32[4,128]{1,0:T(4,128)} %bitcast.1, bf16[256,384]{1,0:T(8,128)(2,1)} %constant.6.clone.main_ref, bf16[64,768]{1,0:T(8,128)(2,1)} %constant.7.clone.halo_ref, ...), custom_call_target="tpu_custom_call" | custom-call | tf_op jit(solution)/shard_map/pallas_call | solution.py:331
  41.4 0.8 %copy.9 = f32[16,2,4096]{2,1,0:T(2,128)} copy(f32[16,2,4096]{2,1,0:T(2,128)S(1)} %shard_map.73) | data formatting | bytes 1048576

commit v6 on v5

--- a/solution.py
+++ b/solution.py
@@ -322,7 +322,8 @@
 def on_device(envelope, mode_profile, dispersion, kerr_gain):
     count = lax.axis_size("mode")
     peers = [(dy, dz, dc) for dy in range(4) for dz in (2, 1, 3, 0) for dc in range(2) if (dy, dz, dc) != (0, 0, 0)]
-    peers.sort(key=lambda d: (d[0] // 2, -min(d[1], 4 - d[1])))
+    rank = {(0, 2): 0, (0, 1): 1, (1, 2): 2, (0, 0): 3, (1, 1): 4, (1, 0): 5}
+    peers.sort(key=lambda d: rank[d[0] // 2, min(d[1], 4 - d[1])])
     n = len(peers)
     modes, grid = mode_profile.shape
     consts = [jnp.asarray(c) for c in constants()]

time: 42.2 us -> 42.2 us (level)
  no operation moved by 1% of the time
where the time goes in v6:
time: 42.2 us
  Pallas kernels  41.3 us (98%)
  local copies, waits for them, and re-layouts  0.8 us (2%)
    pallas_call x1, Pallas kernels, on_device(): pl.pallas_call(functools.partial(kernel, peers, count), out_shape=pltpu.V...  41.3 us

profile of v6, /device:TPU:1, one launch (start us, length us, event | category | flops | bytes accessed | tf_op | source)
XLA Modules:
  0.0 42.2 jit_solution(5497365396123182487)
XLA Ops:
  0.0 41.3 %shard_map.73 = f32[16,2,4096]{2,1,0:T(2,128)S(1)} custom-call(bf16[16,2,4096]{2,1,0:T(2,128)(2,1)} %env_ref.1, bf16[512,8192]{1,0:T(8,128)(2,1)} %prof_ref.1, f32[3,16]{1,0:T(4,128)} %disp_ref.1, f32[4,128]{1,0:T(4,128)} %bitcast.1, bf16[256,384]{1,0:T(8,128)(2,1)} %constant.6.clone.main_ref, bf16[64,768]{1,0:T(8,128)(2,1)} %constant.7.clone.halo_ref, ...), custom_call_target="tpu_custom_call" | custom-call | tf_op jit(solution)/shard_map/pallas_call | solution.py:332
  41.4 0.8 %copy.9 = f32[16,2,4096]{2,1,0:T(2,128)} copy(f32[16,2,4096]{2,1,0:T(2,128)S(1)} %shard_map.73) | data formatting | bytes 1048576
